TPU v7x, 512 devices: a whole 4x8x8 slice. The times are simulated.
512 devices in a mesh: ctx: 16 (over z, core), head: 8 (over y), dp: 4 (over x).
Axes of the slice: x: 4, y: 8, z: 8, core: 2. Of those that a mesh axis runs over, the one named last changes fastest.
Arguments:
- positions: int32 [4, 2048], P('dp', 'ctx'), may hold values from 0 to 2047, as said below
- unnormed_latent: bfloat16 [4, 2048, 512], P('dp', 'ctx'), may hold values from -6 to 6
- latent_norm_gain: float32 [512], replicated, may hold values from 0.5 to 1.5
- key_rope: bfloat16 [4, 2048, 64], P('dp', 'ctx'), may hold values from -9 to 9
- query_nope: bfloat16 [4, 2048, 8192], P('dp', 'ctx', 'head'), may hold values from -6 to 6
- query_rope: bfloat16 [4, 2048, 4096], P('dp', 'ctx', 'head'), may hold values from -48 to 48
- key_up: bfloat16 [64, 128, 512], P('head'), may hold values from -0.5 to 0.5
- value_up: bfloat16 [64, 128, 512], P('head'), may hold values from -0.5 to 0.5
- grad_out: bfloat16 [4, 2048, 8192], P('dp', 'ctx', 'head'), may hold values from -0.75 to 0.75
Outputs:
- raw_latent_gradient: float32 [4, 2048, 512], P('dp', ('ctx', 'head'))
- rope_grad: float32 [4, 2048, 64], P('dp', ('ctx', 'head'))
- norm_gain_gradient: float32 [512], replicated
Inputs may be any that keep to these rules, and one draw needn't show every extreme that they name: In each sequence every position 0 to 2047 stands once. The 128 rows of one index of ctx are two runs of 64 consecutive positions in increasing order: the first starts at 64 * j for some j below 16, the second at 2048 - 64 * (j + 1); which j falls to which index is drawn.
All inputs are finite; a program needn't handle non-finite values.
Results may differ from a plain program's by a relative error of at most 0.04.
Values may be sent and summed in bfloat16 or wider, within the bound.
A program may use at most 64 MiB of HBM per device.

v0:
```python
import math

import jax
import jax.numpy as jnp
from jax import lax
from jax.sharding import PartitionSpec as P


def attend(
    query_latent, query_rotary, out_latent, query_pos, latent_keys, rotary_keys, key_pos, scale
):
    scores = jnp.einsum("rl,kl->rk", query_latent, latent_keys, preferred_element_type=jnp.float32)
    scores = scores + jnp.einsum(
        "rq,kq->rk", query_rotary, rotary_keys, preferred_element_type=jnp.float32
    )
    visible = key_pos[None, :] <= query_pos[:, None]
    scores = jnp.where(visible, scores * scale, -jnp.inf)
    top = jnp.max(scores, axis=1, keepdims=True)
    weights = jnp.exp(scores - top)
    probs = weights / jnp.sum(weights, axis=1, keepdims=True)
    dprob = jnp.einsum("rl,kl->rk", out_latent, latent_keys, preferred_element_type=jnp.float32)
    delta = jnp.sum(probs * dprob, axis=1, keepdims=True)
    dscore = probs * (dprob - delta) * scale
    probs_b = probs.astype(jnp.bfloat16)
    dscore_b = dscore.astype(jnp.bfloat16)
    lat_terms = jnp.einsum("rk,rl->kl", probs_b, out_latent, preferred_element_type=jnp.float32)
    lat_terms = lat_terms + jnp.einsum(
        "rk,rl->kl", dscore_b, query_latent, preferred_element_type=jnp.float32
    )
    rope_terms = jnp.einsum("rk,rq->kq", dscore_b, query_rotary, preferred_element_type=jnp.float32)
    return (lat_terms, rope_terms)


def per_device(
    positions,
    unnormed_latent,
    latent_norm_gain,
    key_rope,
    query_nope,
    query_rope,
    key_up,
    value_up,
    grad_out,
):
    tok = unnormed_latent.shape[1]
    half = tok // 2
    lat_width = unnormed_latent.shape[2]
    rope_width = key_rope.shape[2]
    heads = key_up.shape[0]
    nope = key_up.shape[1]
    val_width = value_up.shape[1]
    scale = float(nope + rope_width) ** (-0.5)
    unnormed_rows = unnormed_latent[0].astype(jnp.float32)
    root_mean_square = jnp.sqrt(
        jnp.mean(unnormed_rows * unnormed_rows, axis=-1, keepdims=True) + 1e-06
    )
    latent_state = (unnormed_rows / root_mean_square * latent_norm_gain).astype(jnp.bfloat16)
    latent_keys, rotary_keys = (
        lax.all_gather(latent_state, "ctx", axis=0, tiled=True),
        lax.all_gather(key_rope[0], "ctx", axis=0, tiled=True),
    )
    key_pos = lax.all_gather(positions[0], "ctx", axis=0, tiled=True)
    shards = latent_keys.shape[0] // tok
    query_latent = jnp.einsum(
        "thd,hdl->thl",
        query_nope[0].reshape(tok, heads, nope),
        key_up,
        preferred_element_type=jnp.float32,
    ).astype(jnp.bfloat16)
    out_latent = jnp.einsum(
        "thv,hvl->thl",
        grad_out[0].reshape(tok, heads, val_width),
        value_up,
        preferred_element_type=jnp.float32,
    ).astype(jnp.bfloat16)
    query_rotary = query_rope[0].reshape(tok, heads, rope_width)
    query_pos = jnp.broadcast_to(positions[0][:, None], (tok, heads))

    def block_rows(values, first):
        return values[first : first + half].reshape((half * heads,) + values.shape[2:])

    upper_lat, upper_rope = attend(
        block_rows(query_latent, half),
        block_rows(query_rotary, half),
        block_rows(out_latent, half),
        block_rows(query_pos, half),
        latent_keys,
        rotary_keys,
        key_pos,
        scale,
    )
    lower_keys = latent_keys.reshape(shards, 2, half, lat_width)[:, 0].reshape(
        shards * half, lat_width
    )
    lower_rotary = rotary_keys.reshape(shards, 2, half, rope_width)[:, 0].reshape(
        shards * half, rope_width
    )
    lower_pos = key_pos.reshape(shards, 2, half)[:, 0].reshape(shards * half)
    lower_lat, lower_rope = attend(
        block_rows(query_latent, 0),
        block_rows(query_rotary, 0),
        block_rows(out_latent, 0),
        block_rows(query_pos, 0),
        lower_keys,
        lower_rotary,
        lower_pos,
        scale,
    )

    def combine(upper, lower, width):
        blocks = upper.reshape(shards, 2, half, width)
        merged = jnp.stack(
            [blocks[:, 0] + lower.reshape(shards, half, width), blocks[:, 1]], axis=1
        )
        rounded = lax.optimization_barrier(merged.reshape(shards * tok, width).astype(jnp.bfloat16))
        return rounded.astype(jnp.float32)

    lat_part = combine(upper_lat, lower_lat, lat_width)
    rope_part = combine(upper_rope, lower_rope, rope_width)
    head_count = lax.axis_size("head")
    piece = tok // head_count
    local_latent_rows, rope_mine = (
        lax.psum_scatter(
            lat_part.astype(jnp.bfloat16), "ctx", scatter_dimension=0, tiled=True
        ).astype(jnp.float32),
        lax.psum_scatter(
            rope_part.astype(jnp.bfloat16), "ctx", scatter_dimension=0, tiled=True
        ).astype(jnp.float32),
    )
    local_latent_rows, rope_mine = (
        lax.psum_scatter(
            local_latent_rows.astype(jnp.bfloat16), "head", scatter_dimension=0, tiled=True
        ).astype(jnp.float32),
        lax.psum_scatter(
            rope_mine.astype(jnp.bfloat16), "head", scatter_dimension=0, tiled=True
        ).astype(jnp.float32),
    )
    local_unnormed_rows = lax.dynamic_slice_in_dim(
        unnormed_rows, lax.axis_index("head") * piece, piece, 0
    )
    local_root_square = jnp.sqrt(
        jnp.mean(local_unnormed_rows * local_unnormed_rows, axis=-1, keepdims=True) + 1e-06
    )
    local_normalized = local_unnormed_rows / local_root_square
    scaled_latent = latent_norm_gain * local_latent_rows
    raw_latent_gradient = (
        scaled_latent
        - local_normalized * jnp.mean(scaled_latent * local_normalized, axis=-1, keepdims=True)
    ) / local_root_square
    gain_gradient_pieces = jnp.sum(local_latent_rows * local_normalized, axis=0)
    gain_total = lax.psum(gain_gradient_pieces, ("ctx", "head", "dp"))
    count = lax.axis_size("ctx") * tok * lax.axis_size("dp")
    norm_gain_gradient = gain_total / math.sqrt(count)
    return (raw_latent_gradient[None], rope_mine[None], norm_gain_gradient)


def solution(mesh):
    in_specs = (
        P("dp", "ctx"),
        P("dp", "ctx", None),
        P(),
        P("dp", "ctx", None),
        P("dp", "ctx", "head"),
        P("dp", "ctx", "head"),
        P("head", None, None),
        P("head", None, None),
        P("dp", "ctx", "head"),
    )
    out_specs = (P("dp", ("ctx", "head"), None), P("dp", ("ctx", "head"), None), P())
    return jax.shard_map(
        per_device, mesh=mesh, in_specs=in_specs, out_specs=out_specs, check_vma=False
    )
```

profile of v0, /device:TPU:1, one launch (start us, length us, event | category | flops | bytes accessed | tf_op | source)
XLA Modules:
  0.0 407.0 jit_solution(14919161192959000120)
XLA Ops:
  7.2 1.1 fusion.49
  8.4 1.7 fusion.51
  10.1 24.6 %all-gather = s32[1,2048]{1,0:T(1,128)S(1)} all-gather(s32[1,128]{1,0:T(1,128)} %param.9), channel_id=2, replica_groups=mesh['ctx'=16,'head'=8,'dp'=4] {'ctx'}, dimensions={1}, use_global_device_ids=true | all-gather | bytes 8704 | tf_op jit(solution)/shard_map/all_gather | solution.py:62
  34.7 0.5 broadcast.103
  35.2 0.7 reduce.9
  36.0 0.8 slice_bitcast_fusion.1
  37.1 0.7 le.47
  37.8 0.9 fusion.72
  38.9 1.0 copy.37
  40.0 15.5 %all-gather.1 = bf16[1,2048,64]{1,2,0:T(8,128)(2,1)S(1)} all-gather(bf16[1,128,64]{1,2,0:T(8,128)(2,1)S(1)} %copy-done.23), channel_id=3, replica_groups=mesh['ctx'=16,'head'=8,'dp'=4] {'ctx'}, dimensions={1}, use_global_device_ids=true | all-gather | bytes 278528 | tf_op jit(solution)/shard_map/all_gather | solution.py:60
  55.5 0.5 reshape.96
  56.0 1.5 slice_reduce_fusion
  58.1 1.1 fusion.71
  59.6 1.1 fusion.70
  60.7 1.8 fusion.73
  62.5 1.4 slice.79
  63.9 0.5 copy-done.2
  64.4 2.0 fusion.18
  66.4 0.6 fusion.20
  67.0 0.4 copy-done.14
  67.5 1.1 multiply_reduce_fusion.1
  68.6 2.6 fusion.26
  71.2 1.7 fusion.10
  73.0 2.3 copy.29
  75.3 3.1 fusion.38
  78.4 1.1 fusion.5
  79.5 1.0 fusion.7
  80.5 0.5 copy-done.13
  81.0 3.8 fusion.15
  84.8 1.7 multiply_reduce_fusion
  86.6 2.0 copy-done.4
  88.5 2.7 fusion.1
  91.3 3.9 copy.26
  95.2 2.4 fusion.55
  98.1 0.9 pad_maximum_fusion.1
  99.4 7.5 %convolution_add_fusion = f32[2048,512]{1,0:T(8,128)S(1)} fusion(f32[2048,512]{1,0:T(8,128)} %fusion.15, f32[512,2048]{1,0:T(8,128)} %copy-done.4, f32[512]{0:T(512)S(1)} %get-tuple-element.15, bf16[64,8,512]{2,0,1:T(8,128)(2,1)} %get-tuple-element.6, f32[512,2048]{1,0:T(8,128)} %copy-done.1, f32[512]{0:T(512)S(1)} %fusion.7, f32[512]{0:T(512)S(1)} %copy-done.21, ...), kind=kOutput, calls=%fused_computation.13 | convolution fusion | flops 1083179008 | bytes 17317888 | tf_op jit(solution)/shard_map/rk,rl->kl/dot_general | solution.py:27
  107.0 1.7 convolution_add_fusion.1
  108.8 0.6 fusion.8
  109.4 1.5 pad_maximum_fusion
  111.0 42.3 %reduce-scatter.9.cloned.1.call-done = bf16[128,64]{1,0:T(8,128)(2,1)} async-done(((bf16[2048,64]{1,0:T(8,128)(2,1)}), bf16[128,64]{1,0:T(8,128)(2,1)}) %reduce-scatter.9.cloned.1.call-update) | async-done | bytes 16400 | tf_op jit(solution)/shard_map/reduce_scatter | solution.py:126
  153.5 63.4 %reduce-scatter.5.cloned.1.call-done = bf16[128,512]{1,0:T(8,128)(2,1)} async-done(((bf16[2048,512]{1,0:T(8,128)(2,1)}), bf16[128,512]{1,0:T(8,128)(2,1)}) %reduce-scatter.5.cloned.1.call-update) | async-done | bytes 131088 | tf_op jit(solution)/shard_map/reduce_scatter | solution.py:123
  217.0 36.9 %reduce-scatter.11.cloned.1.call-done = bf16[16,64]{1,0:T(8,128)(2,1)} async-done(((bf16[128,64]{1,0:T(8,128)(2,1)}), bf16[16,64]{1,0:T(8,128)(2,1)}) %reduce-scatter.11.cloned.1.call-update) | async-done | bytes 2064 | tf_op jit(solution)/shard_map/reduce_scatter | solution.py:134
  253.8 1.3 bitcast_convert_fusion
  255.1 39.3 %reduce-scatter.7.cloned.1.call-done = bf16[16,512]{1,0:T(8,128)(2,1)} async-done(((bf16[128,512]{1,0:T(8,128)(2,1)}), bf16[16,512]{1,0:T(8,128)(2,1)}) %reduce-scatter.7.cloned.1.call-update) | async-done | bytes 16400 | tf_op jit(solution)/shard_map/reduce_scatter | solution.py:131
  294.4 0.9 fusion.62
  295.3 103.1 %psum.7 = f32[512]{0:T(512)S(1)} all-reduce(f32[512]{0:T(512)S(1)} %get-tuple-element.3), channel_id=1, replica_groups=mesh['ctx'=16,'head'=8,'dp'=4] {'ctx','head','dp'}, use_global_device_ids=true, to_apply=%region_14.15 | all-reduce | flops 512 | bytes 4096 | tf_op jit(solution)/shard_map/psum | solution.py:151
  398.5 0.6 broadcast_multiply_fusion
  399.0 1.4 fusion.61
  (85 shorter events, 3.2 us)
Async XLA Ops:
  7.2 50.5 %copy-start = (bf16[8,128,512]{2,1,0:T(8,128)(2,1)S(1)}, bf16[8,128,512]{2,1,0:T(8,128)(2,1)}, u32[]{:S(2)}) copy-start(bf16[8,128,512]{2,1,0:T(8,128)(2,1)} %param.16) | copy-start | bytes 3145732
  7.2 32.7 %copy-start.15 = (bf16[1,128,1024]{2,1,0:T(8,128)(2,1)S(1)}, bf16[1,128,1024]{2,1,0:T(8,128)(2,1)}, u32[]{:S(2)}) copy-start(bf16[1,128,1024]{2,1,0:T(8,128)(2,1)} %param.17) | copy-start | bytes 786436
  7.2 32.8 %copy-start.23 = (bf16[1,128,64]{1,2,0:T(8,128)(2,1)S(1)}, bf16[1,128,64]{1,2,0:T(8,128)(2,1)}, u32[]{:S(2)}) copy-start(bf16[1,128,64]{1,2,0:T(8,128)(2,1)} %param.12) | copy-start | bytes 49156
  7.2 55.3 %all-gather.4.cloned.1.call-start = ((), (), s32[]{:S(2)}) async-start(), calls=%async_computation.4 | async-start | bytes 2228224 | tf_op jit(solution)/shard_map/all_gather | solution.py:59
  10.1 143.2 %reduce-scatter.9.cloned.1.call-start = ((), (), s32[]{:S(2)}) async-start(), calls=%async_computation.7 | async-start | bytes 557056 | tf_op jit(solution)/shard_map/reduce_scatter | solution.py:126
  38.8 21.9 %copy-start.10 = (bf16[512,64]{1,0:T(8,128)(2,1)}, bf16[512,64]{1,0:T(8,128)(2,1)S(1)}, u32[]{:S(2)}) copy-start(bf16[512,64]{1,0:T(8,128)(2,1)S(1)} %reshape.95) | copy-start | bytes 196612
  57.7 1.5 copy-start.12
  62.5 1.9 copy-start.2
  66.4 4.8 %copy-start.18 = (f32[512]{0:T(512)}, f32[512]{0:T(512)S(1)}, u32[]{:S(2)}) copy-start(f32[512]{0:T(512)S(1)} %get-tuple-element.17) | copy-start | bytes 6148
  66.4 1.0 copy-start.14
  67.0 4.2 %copy-start.24 = (f32[512]{0:T(512)}, f32[512]{0:T(512)S(1)}, u32[]{:S(2)}) copy-start(f32[512]{0:T(512)S(1)} %fusion.20) | copy-start | bytes 6148
  68.6 2.6 copy-start.6
  68.6 2.6 copy-start.26
  75.3 3.1 copy-start.16
  79.5 7.0 %copy-start.1 = (f32[512,2048]{1,0:T(8,128)}, f32[512,2048]{1,0:T(8,128)S(1)}, u32[]{:S(2)}) copy-start(f32[512,2048]{1,0:T(8,128)S(1)} %get-tuple-element.14) | copy-start | bytes 12582916
  79.5 7.0 %copy-start.20 = (f32[512]{0:T(512)}, f32[512]{0:T(512)S(1)}, u32[]{:S(2)}) copy-start(f32[512]{0:T(512)S(1)} %get-tuple-element.13) | copy-start | bytes 6148
  79.5 1.4 copy-start.13
  81.0 3.8 copy-start.3
  86.5 2.0 copy-start.4
  95.2 2.5 copy-start.5
  95.2 2.5 copy-start.11
  97.6 1.7 copy-start.17
  97.6 1.7 copy-start.21
  99.0 7.9 %copy-start.19 = (f32[512]{0:T(512)S(1)}, f32[512]{0:T(512)}, u32[]{:S(2)}) copy-start(f32[512]{0:T(512)} %copy-done.18) | copy-start | bytes 6148
  99.1 7.9 %copy-start.25 = (f32[512]{0:T(512)S(1)}, f32[512]{0:T(512)}, u32[]{:S(2)}) copy-start(f32[512]{0:T(512)} %copy-done.24) | copy-start | bytes 6148
  99.1 7.9 %copy-start.27 = (f32[512]{0:T(512)S(1)}, f32[512]{0:T(512)}, u32[]{:S(2)}) copy-start(f32[512]{0:T(512)} %copy-done.26) | copy-start | bytes 6148
  99.1 117.9 %reduce-scatter.5.cloned.1.call-start = ((), (), s32[]{:S(2)}) async-start(), calls=%async_computation.5 | async-start | bytes 2228224 | tf_op jit(solution)/shard_map/reduce_scatter | solution.py:123
  99.4 7.6 %copy-start.7 = (f32[512,1024]{1,0:T(8,128)S(1)}, f32[512,1024]{1,0:T(8,128)}, u32[]{:S(2)}) copy-start(f32[512,1024]{1,0:T(8,128)} %copy-done.6) | copy-start | bytes 6291460
  99.4 7.6 %copy-start.8 = (bf16[64,8,512]{2,0,1:T(8,128)(2,1)S(1)}, bf16[64,8,512]{2,0,1:T(8,128)(2,1)}, u32[]{:S(2)}) copy-start(bf16[64,8,512]{2,0,1:T(8,128)(2,1)} %get-tuple-element.5) | copy-start | bytes 1572868
  99.4 7.6 %copy-start.28 = (f32[1024,512]{1,0:T(8,128)S(1)}, f32[1024,512]{1,0:T(8,128)}, u32[]{:S(2)}) copy-start(f32[1024,512]{1,0:T(8,128)} %fusion.26) | copy-start | bytes 6291460
  110.9 42.4 %copy-start.9 = (bf16[1,128,512]{2,1,0:T(8,128)(2,1)S(1)}, bf16[1,128,512]{2,1,0:T(8,128)(2,1)}, u32[]{:S(2)}) copy-start(bf16[1,128,512]{2,1,0:T(8,128)(2,1)} %param.10) | copy-start | bytes 393220
  110.9 183.5 %copy-start.22 = (f32[512]{0:T(512)S(1)}, f32[512]{0:T(512)}, u32[]{:S(2)}) copy-start(f32[512]{0:T(512)} %param.11) | copy-start | bytes 6148
  111.0 142.9 %reduce-scatter.11.cloned.1.call-start = ((), (), s32[]{:S(2)}) async-start(), calls=%async_computation.8 | async-start | bytes 36864 | tf_op jit(solution)/shard_map/reduce_scatter | solution.py:134
  153.3 141.1 %reduce-scatter.7.cloned.1.call-start = ((), (), s32[]{:S(2)}) async-start(), calls=%async_computation.6 | async-start | bytes 147456 | tf_op jit(solution)/shard_map/reduce_scatter | solution.py:131
Sparse Core Ops, SparseCore 0:
  10.2 49.0 all-gather.3
  99.2 54.0 reduce-scatter.8
  156.4 60.5 reduce-scatter.4
  219.8 34.0 reduce-scatter.10
  256.5 37.8 reduce-scatter.6
where the time goes:
time: 408 us; the launch traced here: 407 us
  waiting for transfers between devices  182 us (45%)
  blocking collectives  143 us (35%)
  matrix products  30.2 us (7%)
  local copies, waits for them, and re-layouts  20.2 us (5%)
  other arithmetic  16.9 us (4%)
  between operations  14.2 us (3%)
    psum x1, blocking collectives, per_device(): gain_total = lax.psum(gain_gradient_pieces, ('ctx', 'head', 'dp'))  103 us
    reduce_scatter x1, waiting for transfers between devices, per_device(): lax.psum_scatter(lat_part.astype(jnp.bfloat16), 'ctx', scatter_dimension=...  63.4 us
    reduce_scatter x1, waiting for transfers between devices, per_device(): lax.psum_scatter(rope_part.astype(jnp.bfloat16), 'ctx', scatter_dimension...  42.3 us
    reduce_scatter x1, waiting for transfers between devices, per_device(): lax.psum_scatter(local_latent_rows.astype(jnp.bfloat16), 'head', scatter_...  39.3 us
    reduce_scatter x1, waiting for transfers between devices, per_device(): lax.psum_scatter(rope_mine.astype(jnp.bfloat16), 'head', scatter_dimensio...  36.9 us
    all_gather x1, blocking collectives, per_device(): key_pos = lax.all_gather(positions[0], 'ctx', axis=0, tiled=True)  24.6 us
    all_gather x1, blocking collectives, per_device(): lax.all_gather(key_rope[0], 'ctx', axis=0, tiled=True)  15.5 us
    dot_general x2, matrix products, attend(): jnp.einsum('rk,rl->kl', dscore_b, query_latent, preferred_element_type=jn...  9.2 us
  transfers between devices with their start and end apart: 5, of which 4 were waited for; matrix products, arithmetic and copies ran while one was open for 6% of the time, Pallas kernels for 0%

commit v1 on v0

v1 whole, which is shorter than its diff:
```python
import functools
import math

import jax
import jax.numpy as jnp
from jax import lax
from jax.experimental import pallas as pl
from jax.experimental.pallas import tpu as pltpu
from jax.sharding import PartitionSpec as P

BF16 = jnp.bfloat16
F32 = jnp.float32
MESH = pl.DeviceIdType.MESH


def dot(a, b):
    return jnp.dot(a, b, preferred_element_type=F32)


def dot_t(a, b):
    return lax.dot_general(a, b, (((1,), (1,)), ((), ())), preferred_element_type=F32)


def kernel(
    nz, ny, nx, total_rows,
    pos_ref, x_ref, gain_ref, kr_ref, qn_ref, qr_ref, ku_ref, vu_ref, go_ref,
    raw_ref, rope_ref, gout_ref,
    keys, posbuf, qlat, olat, qrp, wbuf, dbuf, diff,
    pown, psib, rsib, sendp, recvp, sendm, recvm, ysend, yrecv, gsend, gx, gy, gc,
    sem_as, sem_ar, sem_ps, sem_pr, sem_ss, sem_sr, sem_zs, sem_zr, sem_ys, sem_yr, sem_gs, sem_gr,
):
    nc = 2 * nz
    half_z = nz // 2
    me = lax.axis_index("ctx")
    y = lax.axis_index("head")
    x = lax.axis_index("dp")
    z = me // 2
    c = lax.rem(me, 2)
    sib = z * 2 + (1 - c)
    up = lax.rem(z + 1, nz) * 2 + c
    down = lax.rem(z + nz - 1, nz) * 2 + c

    def at_z(off):
        return lax.rem(z + off + nz, nz)

    def rem_copy(src, dst, ssem, rsem, dev):
        return pltpu.make_async_remote_copy(
            src_ref=src, dst_ref=dst, send_sem=ssem, recv_sem=rsem, device_id=dev, device_id_type=MESH
        )

    barrier = pltpu.get_barrier_semaphore()
    for d in range(1, nc):
        pl.semaphore_signal(barrier, inc=1, device_id={"ctx": lax.rem(me + d, nc)}, device_id_type=MESH)
    for d in range(1, ny):
        pl.semaphore_signal(barrier, inc=1, device_id={"head": lax.rem(y + d, ny)}, device_id_type=MESH)
    for d in range(1, nx):
        pl.semaphore_signal(barrier, inc=1, device_id={"dp": lax.rem(x + d, nx)}, device_id_type=MESH)

    rows = x_ref[0].astype(F32)
    rms = jnp.sqrt(jnp.mean(rows * rows, axis=-1, keepdims=True) + 1e-06)
    keys[me, 0:128, :] = (rows / rms * gain_ref[...]).astype(BF16)
    ri = lax.broadcasted_iota(jnp.int32, (64, 128), 0)
    ci = lax.broadcasted_iota(jnp.int32, (64, 128), 1)
    packed = dot(kr_ref[0, 0:64, :], (ci == ri).astype(BF16)) + dot(
        kr_ref[0, 64:128, :], (ci == ri + 64).astype(BF16)
    )
    packed = packed.astype(BF16)
    for g in range(4):
        keys[me, 128:144, 128 * g : 128 * g + 128] = packed[16 * g : 16 * g + 16]
    posbuf[me] = jnp.broadcast_to(pos_ref[...], (8, 128))

    pl.semaphore_wait(barrier, (nc - 1) + (ny - 1) + (nx - 1))

    started = []

    def start(copy):
        copy.start()
        started.append(copy)

    def gather_copy(block, way, index):
        dev = (up, down, sib)[way]
        return rem_copy(
            keys.at[block], keys.at[block], sem_as.at[way, index], sem_ar.at[way, index], {"ctx": dev}
        )

    def pos_copy(d, slot):
        return rem_copy(
            posbuf.at[slot], posbuf.at[slot], sem_ps.at[d], sem_pr.at[d], {"ctx": lax.rem(me + d, nc)}
        )

    start(gather_copy(me, 0, 1))
    if half_z > 1:
        start(gather_copy(me, 1, 1))
    start(gather_copy(me, 2, 0))
    for d in range(1, nc):
        start(pos_copy(d, me))

    fi = lax.broadcasted_iota(jnp.int32, (128, 128), 0)
    fj = lax.broadcasted_iota(jnp.int32, (128, 128), 1)
    for h in range(8):
        part = dot(qn_ref[0, :, 128 * h : 128 * h + 128], ku_ref[h]).astype(BF16)
        qlat[0, 64 * h : 64 * h + 64, :] = part[0:64]
        qlat[1, 64 * h : 64 * h + 64, :] = part[64:128]
        part = dot(go_ref[0, :, 128 * h : 128 * h + 128], vu_ref[h]).astype(BF16)
        olat[0, 64 * h : 64 * h + 64, :] = part[0:64]
        olat[1, 64 * h : 64 * h + 64, :] = part[64:128]
        pair = qr_ref[0, :, 128 * (h // 2) : 128 * (h // 2) + 128]
        e = 64 * (h % 2)
        left = dot(pair, ((fi == fj + e) & (fj < 64)).astype(BF16)).astype(BF16)
        right = dot(pair[64:128], ((fi + 64 - e == fj) & (fj >= 64)).astype(BF16)).astype(BF16)
        qrp[0, 64 * h : 64 * h + 64, :] = left[0:64]
        qrp[1, 64 * h : 64 * h + 64, :] = left[64:128]
        qrp[2, 64 * h : 64 * h + 64, :] = right
    diff[...] = lax.rem(lax.broadcasted_iota(jnp.int32, (64, 512), 1), 64) - lax.broadcasted_iota(
        jnp.int32, (64, 512), 0
    )

    scale = float(128 + 64) ** (-0.5)
    to_log2 = scale * math.log2(math.e)

    groups = [[0]] + [[t, -t] for t in range(1, half_z)] + [[half_z]]
    first = []
    count = 0
    for g in groups:
        first.append(count)
        count += 2 * len(g)

    def blocks_of(g):
        return [at_z(off) * 2 + cc for off in g for cc in range(2)]

    def cat(parts):
        return parts[0] if len(parts) == 1 else jnp.concatenate(parts, axis=0)

    def rope_rows(b):
        return [keys[b, 128:144, 128 * g : 128 * g + 128] for g in range(4)]

    m_up = jnp.full((1, 512), -jnp.inf, F32)
    m_lo = m_up
    l_up = jnp.zeros((1, 512), F32)
    l_lo, d_up, d_lo = l_up, l_up, l_up
    tops = []
    for t, g in enumerate(groups):
        if t == 0:
            for d in range(1, nc):
                pos_copy(d, lax.rem(me - d + nc, nc)).wait_recv()
        else:
            block = at_z(-t) * 2 + c
            gather_copy(block, 0, t).wait_recv()
            if t < half_z:
                start(gather_copy(block, 0, t + 1))
            start(gather_copy(block, 2, t))
            if t < half_z:
                block = at_z(t) * 2 + c
                gather_copy(block, 1, t).wait_recv()
                if t + 1 < half_z:
                    start(gather_copy(block, 1, t + 1))
                start(gather_copy(block, 2, half_z + t))
        other = 1 - c
        gather_copy(at_z(-t) * 2 + other, 2, t).wait_recv()
        if 0 < t < half_z:
            gather_copy(at_z(t) * 2 + other, 2, half_z + t).wait_recv()

        blocks = blocks_of(g)
        n = 64 * len(blocks)
        span = pl.ds(64 * first[t], n)
        low = cat([keys[b, 0:64, :] for b in blocks])
        high = cat([keys[b, 64:128, :] for b in blocks])
        rope = cat([r for b in blocks for r in rope_rows(b)])
        wbuf[0, span, :] = (dot_t(low, qlat[1]) + dot_t(rope, qrp[1])) * to_log2
        dbuf[0, span, :] = dot_t(low, olat[1])
        s_high = (dot_t(high, qlat[1]) + dot_t(rope, qrp[2])) * to_log2
        dbuf[1, span, :] = dot_t(high, olat[1])
        s_low = (dot_t(low, qlat[0]) + dot_t(rope, qrp[0])) * to_log2
        dbuf[2, span, :] = dot_t(low, olat[0])
        for i, b in enumerate(blocks):
            sub = pl.ds(64 * (first[t] + i), 64)
            late = posbuf[b, 0:1, 64:65] - pos_ref[0:1, 64:65]
            early = posbuf[b, 0:1, 0:1] - pos_ref[0:1, 0:1]
            wbuf[1, sub, :] = jnp.where(diff[...] >= late, s_high[64 * i : 64 * i + 64], -jnp.inf)
            wbuf[2, sub, :] = jnp.where(diff[...] >= early, s_low[64 * i : 64 * i + 64], -jnp.inf)
        new_up = jnp.maximum(
            m_up,
            jnp.maximum(
                jnp.max(wbuf[0, span, :], axis=0, keepdims=True), jnp.max(wbuf[1, span, :], axis=0, keepdims=True)
            ),
        )
        new_lo = jnp.maximum(m_lo, jnp.max(wbuf[2, span, :], axis=0, keepdims=True))
        a_up = jnp.exp2(m_up - new_up)
        a_lo = jnp.exp2(m_lo - new_lo)
        m_up, m_lo = new_up, new_lo
        l_up, d_up, l_lo, d_lo = l_up * a_up, d_up * a_up, l_lo * a_lo, d_lo * a_lo
        tops.append((m_up, m_lo))
        for kind in range(3):
            top = m_lo if kind == 2 else m_up
            w = jnp.exp2(wbuf[kind, span, :] - top)
            wbuf[kind, span, :] = w
            l_add = jnp.sum(w, axis=0, keepdims=True)
            d_add = jnp.sum(w * dbuf[kind, span, :], axis=0, keepdims=True)
            if kind == 2:
                l_lo, d_lo = l_lo + l_add, d_lo + d_add
            else:
                l_up, d_up = l_up + l_add, d_up + d_add

    inv_up, inv_lo = 1.0 / l_up, 1.0 / l_lo
    delta_up, delta_lo = d_up * inv_up, d_lo * inv_lo

    def sib_copy(index):
        return rem_copy(
            psib.at[index], rsib.at[index], sem_ss.at[index], sem_sr.at[index], {"ctx": sib}
        )

    def ring_copy(way, step):
        src, dst, dev = ((sendp, recvp, up), (sendm, recvm, down))[way]
        return rem_copy(
            src.at[step], dst.at[step], sem_zs.at[way, step], sem_zr.at[way, step], {"ctx": dev}
        )

    index_of = {off: i for i, off in enumerate(off for g in groups for off in g)}

    def summed(off):
        i = index_of[off]
        return pown[i].astype(F32) + rsib[i].astype(F32)

    def send_on(t):
        for off in groups[t]:
            sib_copy(index_of[off]).wait_recv()
        step = half_z - t
        total = summed(t)
        if step > 0:
            ring_copy(0, step - 1).wait_recv()
            total = total + recvp[step - 1].astype(F32)
        sendp[step] = total.astype(BF16)
        start(ring_copy(0, step))
        if t < half_z:
            step = half_z - 1 - t
            total = summed(-t)
            if step > 0:
                ring_copy(1, step - 1).wait_recv()
                total = total + recvm[step - 1].astype(F32)
            sendm[step] = total.astype(BF16)
            start(ring_copy(1, step))

    gain_acc = jnp.zeros((1, 512), F32)
    for t in reversed(range(len(groups))):
        g = groups[t]
        blocks = blocks_of(g)
        n = 64 * len(blocks)
        span = pl.ds(64 * first[t], n)
        c_up = jnp.exp2(tops[t][0] - m_up) * inv_up
        c_lo = jnp.exp2(tops[t][1] - m_lo) * inv_lo
        probs = []
        dscores = []
        for kind in range(3):
            factor, delta = (c_lo, delta_lo) if kind == 2 else (c_up, delta_up)
            p = wbuf[kind, span, :] * factor
            probs.append(p.astype(BF16))
            dscores.append((p * (dbuf[kind, span, :] - delta) * scale).astype(BF16))
        lat_low = (
            dot(probs[0], olat[1]) + dot(dscores[0], qlat[1]) + dot(probs[2], olat[0]) + dot(dscores[2], qlat[0])
        )
        lat_high = dot(probs[1], olat[1]) + dot(dscores[1], qlat[1])
        rope = dot(dscores[0], qrp[1]) + dot(dscores[1], qrp[2]) + dot(dscores[2], qrp[0])
        low = cat([keys[b, 0:64, :] for b in blocks])
        high = cat([keys[b, 64:128, :] for b in blocks])
        gain_acc = gain_acc + jnp.sum(
            lat_low * low.astype(F32) + lat_high * high.astype(F32), axis=0, keepdims=True
        )
        lat_low = lat_low.astype(BF16)
        lat_high = lat_high.astype(BF16)
        rope = rope.astype(BF16)
        for i, b in enumerate(blocks):
            index = index_of[g[i // 2]]

            def put(buf):
                buf[index, 0:64, :] = lat_low[64 * i : 64 * i + 64]
                buf[index, 64:128, :] = lat_high[64 * i : 64 * i + 64]
                for k in range(4):
                    buf[index, 128:144, 128 * k : 128 * k + 128] = rope[64 * i + 16 * k : 64 * i + 16 * k + 16]

            @pl.when(c == i % 2)
            def _():
                put(pown)

            @pl.when(c != i % 2)
            def _():
                put(psib)

        for off in g:
            start(sib_copy(index_of[off]))
        if t < half_z:
            send_on(t + 1)

    gsend[0] = gain_acc

    def gain_copy(stage, d, slot):
        buf, base, axis, pos, size = (
            (gx, 0, "dp", x, nx), (gy, nx - 1, "head", y, ny), (gc, nx + ny - 2, "ctx", me, nc)
        )[stage]
        return rem_copy(
            gsend.at[stage], buf.at[slot], sem_gs.at[base + d - 1], sem_gr.at[base + d - 1],
            {axis: lax.rem(pos + d, size)},
        )

    def gain_send(stage):
        buf, pos, size = ((gx, x, nx), (gy, y, ny), (gc, me, nc))[stage]
        buf[pos] = gsend[stage]
        for d in range(1, size):
            start(gain_copy(stage, d, pos))

    def gain_sum(stage):
        buf, pos, size = ((gx, x, nx), (gy, y, ny), (gc, me, nc))[stage]
        for d in range(1, size):
            gain_copy(stage, d, lax.rem(pos - d + size, size)).wait_recv()
        return jnp.sum(buf[...], axis=0)

    gain_send(0)
    gsend[1] = gain_sum(0)
    gain_send(1)

    sib_copy(0).wait_recv()
    total = summed(0)
    ring_copy(0, half_z - 1).wait_recv()
    total = total + recvp[half_z - 1].astype(F32)
    if half_z > 1:
        ring_copy(1, half_z - 2).wait_recv()
        total = total + recvm[half_z - 2].astype(F32)
    for k in range(ny):
        q = k % 4
        ysend[k, :, 0:512] = total[16 * k : 16 * k + 16, :].astype(BF16)
        ysend[k, :, 512:640] = total[128:144, 128 * q : 128 * q + 128].astype(BF16)

    def y_copy(d, slot):
        peer = lax.rem(y + d, ny)
        return rem_copy(
            ysend.at[peer], yrecv.at[slot], sem_ys.at[d - 1], sem_yr.at[d - 1], {"head": peer}
        )

    for d in range(1, ny):
        start(y_copy(d, y))
    yrecv[y] = ysend[y]
    gsend[2] = gain_sum(1)
    gain_send(2)
    for d in range(1, ny):
        y_copy(d, lax.rem(y - d + ny, ny)).wait_recv()
    mine = jnp.sum(yrecv[...].astype(F32), axis=0)

    cot = mine[:, 0:512]
    own = x_ref[0, pl.ds(pl.multiple_of(16 * y, 16), 16), :].astype(F32)
    own_rms = jnp.sqrt(jnp.mean(own * own, axis=-1, keepdims=True) + 1e-06)
    xhat = own / own_rms
    scaled = gain_ref[...] * cot
    raw_ref[0] = (scaled - xhat * jnp.mean(scaled * xhat, axis=-1, keepdims=True)) / own_rms
    both = mine[:, 512:640]
    rope_ref[0] = jnp.where(y >= ny // 2, pltpu.roll(both, 64, 1), both)[:, 0:64]

    gout_ref[...] = gain_sum(2) / gain_ref[...] * (1.0 / math.sqrt(total_rows))
    for copy in started:
        copy.wait_send()


def solution(mesh):
    nc, ny, nx = mesh.shape["ctx"], mesh.shape["head"], mesh.shape["dp"]
    nz = nc // 2
    half_z = nz // 2

    def per_device(pos, unnormed, gain, kr, qn, qr, ku, vu, go):
        dma = pltpu.SemaphoreType.DMA
        out = pl.pallas_call(
            functools.partial(kernel, nz, ny, nx, nc * 128 * nx),
            out_shape=(
                jax.ShapeDtypeStruct((1, 16, 512), F32),
                jax.ShapeDtypeStruct((1, 16, 64), F32),
                jax.ShapeDtypeStruct((1, 512), F32),
            ),
            in_specs=[pl.BlockSpec(memory_space=pltpu.VMEM)] * 9,
            out_specs=[pl.BlockSpec(memory_space=pltpu.VMEM)] * 3,
            scratch_shapes=[
                pltpu.VMEM((nc, 144, 512), BF16),
                pltpu.VMEM((nc, 8, 128), jnp.int32),
                pltpu.VMEM((2, 512, 512), BF16),
                pltpu.VMEM((2, 512, 512), BF16),
                pltpu.VMEM((3, 512, 128), BF16),
                pltpu.VMEM((3, 64 * nc, 512), F32),
                pltpu.VMEM((3, 64 * nc, 512), F32),
                pltpu.VMEM((64, 512), jnp.int32),
                pltpu.VMEM((nz, 144, 512), BF16),
                pltpu.VMEM((nz, 144, 512), BF16),
                pltpu.VMEM((nz, 144, 512), BF16),
                pltpu.VMEM((half_z, 144, 512), BF16),
                pltpu.VMEM((half_z, 144, 512), BF16),
                pltpu.VMEM((max(half_z - 1, 1), 144, 512), BF16),
                pltpu.VMEM((max(half_z - 1, 1), 144, 512), BF16),
                pltpu.VMEM((ny, 16, 640), BF16),
                pltpu.VMEM((ny, 16, 640), BF16),
                pltpu.VMEM((3, 1, 512), F32),
                pltpu.VMEM((nx, 1, 512), F32),
                pltpu.VMEM((ny, 1, 512), F32),
                pltpu.VMEM((nc, 1, 512), F32),
                dma((3, nz + 1)),
                dma((3, nz + 1)),
                dma((nc,)),
                dma((nc,)),
                dma((nz,)),
                dma((nz,)),
                dma((2, half_z)),
                dma((2, half_z)),
                dma((ny,)),
                dma((ny,)),
                dma((nx + ny + nc,)),
                dma((nx + ny + nc,)),
            ],
            compiler_params=pltpu.CompilerParams(
                collective_id=0, has_side_effects=True, vmem_limit_bytes=52 * 1024 * 1024
            ),
        )(pos, unnormed, gain.reshape(1, 512), kr, qn, qr, ku, vu, go)
        return out[0], out[1], out[2].reshape(512)

    in_specs = (
        P("dp", "ctx"),
        P("dp", "ctx", None),
        P(),
        P("dp", "ctx", None),
        P("dp", "ctx", "head"),
        P("dp", "ctx", "head"),
        P("head", None, None),
        P("head", None, None),
        P("dp", "ctx", "head"),
    )
    out_specs = (P("dp", ("ctx", "head"), None), P("dp", ("ctx", "head"), None), P())
    return jax.shard_map(
        per_device, mesh=mesh, in_specs=in_specs, out_specs=out_specs, check_vma=False
    )
```

time: 408 us -> 84.3 us (0.21)
  waiting for transfers between devices: 182 us -> 0 us
  blocking collectives: 143 us -> 0 us
  Pallas kernels: 0 us -> 75.7 us
  matrix products: 30.2 us -> 0 us
  other arithmetic: 16.9 us -> 0 us
  between operations: 14.2 us -> 0.69 us
  local copies, waits for them, and re-layouts: 20.2 us -> 7.56 us
    reduce_scatter x4 -> x0, waiting for transfers between devices: 182 us -> none  [the longest x1 63.4 us: per_device(): lax.psum_scatter(lat_part.astype(jnp.bfloat16), 'ctx', scatter_dimension=...]
    psum x1 -> x0, blocking collectives: 103 us -> none  [per_device(): gain_total = lax.psum(gain_gradient_pieces, ('ctx', 'head', 'dp'))]
    pallas_call x0 -> x1, Pallas kernels: none -> 75.7 us  [per_device(): pl.pallas_call(functools.partial(kernel, nz, ny, nx, nc * 128 * nx), out_...]
    all_gather x2 -> x0, blocking collectives: 40 us -> none  [the longest x1 24.6 us: per_device(): key_pos = lax.all_gather(positions[0], 'ctx', axis=0, tiled=True)]
    dot_general x14 -> x0, matrix products: 30.2 us -> none  [the longest x2 9.2 us: attend(): jnp.einsum('rk,rl->kl', dscore_b, query_latent, preferred_element_type=jn...]
    slice x9 -> x0, local copies, waits for them, and re-layouts: 6.97 us -> none  [the longest x4 3.85 us: block_rows(): values[first:first + half].reshape((half * heads,) + values.shape[2:])]
    convert_element_type x2 -> x0, local copies, waits for them, and re-layouts: 6.24 us -> none  [attend(): dscore_b = dscore.astype(jnp.bfloat16)]
    convert_element_type x4 -> x0, other arithmetic: 6.2 us -> none  [the longest x2 4.49 us: attend(): dscore_b = dscore.astype(jnp.bfloat16)]
  transfers between devices with their start and end apart: 5 -> 0, of which waited for: 4 -> 0; matrix products, arithmetic and copies ran while one was open for 6% -> 0% of each run, Pallas kernels for 0% -> 0%
where the time goes in v1:
time: 84.3 us; the launch traced here: 83.9 us
  Pallas kernels  75.7 us (90%)
  local copies, waits for them, and re-layouts  7.56 us (9%)
    pallas_call x1, Pallas kernels, per_device(): pl.pallas_call(functools.partial(kernel, nz, ny, nx, nc * 128 * nx), out_...  75.7 us
    unnamed x18, local copies, waits for them, and re-layouts  7.56 us

profile of v1, /device:TPU:1, one launch (start us, length us, event | category | flops | bytes accessed | tf_op | source)
XLA Modules:
  0.0 83.9 jit_solution(7311645704472982620)
XLA Ops:
  0.6 0.0 copy-start.5
  0.6 0.0 copy-start.6
  0.7 0.8 copy.12.kr_ref
  1.5 0.0 copy-done.5
  1.5 0.0 copy-done.6
  1.5 0.0 copy-start
  1.5 1.2 %copy-done = bf16[8,128,512]{2,1,0:T(8,128)(2,1)S(1)} copy-done((bf16[8,128,512]{2,1,0:T(8,128)(2,1)S(1)}, bf16[8,128,512]{2,1,0:T(8,128)(2,1)}, u32[]{:S(2)}) %copy-start) | copy-done | bytes 1048600
  2.7 0.0 copy-start.1
  2.7 0.9 %copy-done.1 = bf16[1,128,1024]{2,1,0:T(8,128)(2,1)S(1)} copy-done((bf16[1,128,1024]{2,1,0:T(8,128)(2,1)S(1)}, bf16[1,128,1024]{2,1,0:T(8,128)(2,1)}, u32[]{:S(2)}) %copy-start.1) | copy-done | bytes 262168
  3.7 0.0 copy-start.2
  3.7 0.9 %copy-done.2 = bf16[1,128,1024]{2,1,0:T(8,128)(2,1)S(1)} copy-done((bf16[1,128,1024]{2,1,0:T(8,128)(2,1)S(1)}, bf16[1,128,1024]{2,1,0:T(8,128)(2,1)}, u32[]{:S(2)}) %copy-start.2) | copy-done | bytes 262168
  4.6 0.0 copy-start.3
  4.6 0.9 %copy-done.3 = bf16[1,128,512]{2,1,0:T(8,128)(2,1)S(1)} copy-done((bf16[1,128,512]{2,1,0:T(8,128)(2,1)S(1)}, bf16[1,128,512]{2,1,0:T(8,128)(2,1)}, u32[]{:S(2)}) %copy-start.3) | copy-done | bytes 131096
  5.5 0.0 copy-start.4
  5.5 0.9 %copy-done.4 = bf16[1,128,512]{2,1,0:T(8,128)(2,1)S(1)} copy-done((bf16[1,128,512]{2,1,0:T(8,128)(2,1)S(1)}, bf16[1,128,512]{2,1,0:T(8,128)(2,1)}, u32[]{:S(2)}) %copy-start.4) | copy-done | bytes 131096
  6.4 75.7 %shard_map.112 = (f32[1,16,512]{2,1,0:T(8,128)S(1)}, f32[1,16,64]{2,1,0:T(8,128)S(1)}, f32[1,512]{1,0:T(1,128)S(1)}) custom-call(s32[1,128]{1,0:T(1,128)S(1)} %copy-done.6, bf16[1,128,512]{2,1,0:T(8,128)(2,1)S(1)} %copy-done.3, f32[1,512]{1,0:T(1,128)S(1)} %bitcast.3, bf16[1,128,64]{2,1,0:T(8,128)(2,1)S(1)} %copy.12.kr_ref, ...), custom_call_target="tpu_custom_call" | custom-call | tf_op jit(solution)/shard_map/pallas_call | solution.py:368
  82.1 0.6 copy.16
  82.7 0.6 copy.17
  83.3 0.6 copy.18
Async XLA Ops:
  0.6 0.9 %copy-start.5 = (f32[512]{0:T(512)S(1)}, f32[512]{0:T(512)}, u32[]{:S(2)}) copy-start(f32[512]{0:T(512)} %param.11) | copy-start | bytes 6148
  0.6 0.9 %copy-start.6 = (s32[1,128]{1,0:T(1,128)S(1)}, s32[1,128]{1,0:T(1,128)}, u32[]{:S(2)}) copy-start(s32[1,128]{1,0:T(1,128)} %pos_ref.1) | copy-start | bytes 1540
  1.5 1.2 %copy-start = (bf16[8,128,512]{2,1,0:T(8,128)(2,1)S(1)}, bf16[8,128,512]{2,1,0:T(8,128)(2,1)}, u32[]{:S(2)}) copy-start(bf16[8,128,512]{2,1,0:T(8,128)(2,1)} %ku_ref.1) | copy-start | bytes 3145732
  2.7 0.9 %copy-start.1 = (bf16[1,128,1024]{2,1,0:T(8,128)(2,1)S(1)}, bf16[1,128,1024]{2,1,0:T(8,128)(2,1)}, u32[]{:S(2)}) copy-start(bf16[1,128,1024]{2,1,0:T(8,128)(2,1)} %qn_ref.1) | copy-start | bytes 786436
  3.7 0.9 %copy-start.2 = (bf16[1,128,1024]{2,1,0:T(8,128)(2,1)S(1)}, bf16[1,128,1024]{2,1,0:T(8,128)(2,1)}, u32[]{:S(2)}) copy-start(bf16[1,128,1024]{2,1,0:T(8,128)(2,1)} %go_ref.1) | copy-start | bytes 786436
  4.6 0.9 %copy-start.3 = (bf16[1,128,512]{2,1,0:T(8,128)(2,1)S(1)}, bf16[1,128,512]{2,1,0:T(8,128)(2,1)}, u32[]{:S(2)}) copy-start(bf16[1,128,512]{2,1,0:T(8,128)(2,1)} %x_ref.1) | copy-start | bytes 393220
  5.5 0.9 %copy-start.4 = (bf16[1,128,512]{2,1,0:T(8,128)(2,1)S(1)}, bf16[1,128,512]{2,1,0:T(8,128)(2,1)}, u32[]{:S(2)}) copy-start(bf16[1,128,512]{2,1,0:T(8,128)(2,1)} %qr_ref.1) | copy-start | bytes 393220

commit v2 on v1

--- a/solution.py
+++ b/solution.py
@@ -23,10 +23,11 @@
 
 def kernel(
     nz, ny, nx, total_rows,
-    pos_ref, x_ref, gain_ref, kr_ref, qn_ref, qr_ref, ku_ref, vu_ref, go_ref,
+    pos_in, x_in, gain_in, kr_in, qn_in, qr_in, ku_in, vu_in, go_in,
     raw_ref, rope_ref, gout_ref,
+    pos_ref, x_ref, gain_ref, kr_ref, qn_ref, qr_ref, ku_ref, vu_ref, go_ref, sem_in,
     keys, posbuf, qlat, olat, qrp, wbuf, dbuf, diff,
-    pown, psib, rsib, sendp, recvp, sendm, recvm, ysend, yrecv, gsend, gx, gy, gc,
+    pown, psib, rsib, zout, zin, yout, yin, yout2, yin2, zout2, zin2, gsend, gx, gy, gc,
     sem_as, sem_ar, sem_ps, sem_pr, sem_ss, sem_sr, sem_zs, sem_zr, sem_ys, sem_yr, sem_gs, sem_gr,
 ):
     nc = 2 * nz
@@ -37,8 +38,6 @@
     z = me // 2
     c = lax.rem(me, 2)
     sib = z * 2 + (1 - c)
-    up = lax.rem(z + 1, nz) * 2 + c
-    down = lax.rem(z + nz - 1, nz) * 2 + c
 
     def at_z(off):
         return lax.rem(z + off + nz, nz)
@@ -47,6 +46,12 @@
         return pltpu.make_async_remote_copy(
             src_ref=src, dst_ref=dst, send_sem=ssem, recv_sem=rsem, device_id=dev, device_id_type=MESH
         )
+
+    ins = (x_in, kr_in, gain_in, pos_in, qn_in, ku_in, go_in, vu_in, qr_in)
+    here = (x_ref, kr_ref, gain_ref, pos_ref, qn_ref, ku_ref, go_ref, vu_ref, qr_ref)
+    loads = [pltpu.make_async_copy(a, b, sem_in.at[i]) for i, (a, b) in enumerate(zip(ins, here))]
+    for load in loads:
+        load.start()
 
     barrier = pltpu.get_barrier_semaphore()
     for d in range(1, nc):
@@ -56,18 +61,22 @@
     for d in range(1, nx):
         pl.semaphore_signal(barrier, inc=1, device_id={"dp": lax.rem(x + d, nx)}, device_id_type=MESH)
 
+    for load in loads[0:4]:
+        load.wait()
     rows = x_ref[0].astype(F32)
     rms = jnp.sqrt(jnp.mean(rows * rows, axis=-1, keepdims=True) + 1e-06)
     keys[me, 0:128, :] = (rows / rms * gain_ref[...]).astype(BF16)
     ri = lax.broadcasted_iota(jnp.int32, (64, 128), 0)
     ci = lax.broadcasted_iota(jnp.int32, (64, 128), 1)
-    packed = dot(kr_ref[0, 0:64, :], (ci == ri).astype(BF16)) + dot(
-        kr_ref[0, 64:128, :], (ci == ri + 64).astype(BF16)
+    rotary = kr_ref[0]
+    none = jnp.zeros_like(rotary)
+    packed = dot_t((ci == ri).astype(BF16), jnp.concatenate([rotary, none], axis=0)) + dot_t(
+        (ci == ri + 64).astype(BF16), jnp.concatenate([none, rotary], axis=0)
     )
     packed = packed.astype(BF16)
     for g in range(4):
         keys[me, 128:144, 128 * g : 128 * g + 128] = packed[16 * g : 16 * g + 16]
-    posbuf[me] = jnp.broadcast_to(pos_ref[...], (8, 128))
+    posbuf[me] = pos_ref[...]
 
     pl.semaphore_wait(barrier, (nc - 1) + (ny - 1) + (nx - 1))
 
@@ -77,26 +86,59 @@
         copy.start()
         started.append(copy)
 
-    def gather_copy(block, way, index):
-        dev = (up, down, sib)[way]
-        return rem_copy(
-            keys.at[block], keys.at[block], sem_as.at[way, index], sem_ar.at[way, index], {"ctx": dev}
-        )
+    offsets = [0] + [off for t in range(1, half_z) for off in (t, -t)] + [half_z]
+    index_of = {off: i for i, off in enumerate(offsets)}
+    far = [off for off in offsets if abs(off) > 1]
+
+    def lanes(row):
+        return pl.ds(pl.multiple_of(128 * lax.rem(row + ny, 4), 128), 128)
+
+    def z_copy(off, owner):
+        i = index_of[off]
+        ref = keys.at[owner] if off not in far else keys.at[owner, :, lanes(y)]
+        return rem_copy(ref, ref, sem_as.at[0, i], sem_ar.at[0, i], {"ctx": at_z(off) * 2 + c})
+
+    def sib_block(off, core):
+        i = index_of[off]
+        ref = keys.at[at_z(off) * 2 + core]
+        return rem_copy(ref, ref, sem_as.at[1, i], sem_ar.at[1, i], {"ctx": sib})
+
+    def y_quarter(off, way, row):
+        i = index_of[off]
+        step = (1, -1, 2 - 4 * c)[way]
+        ref = keys.at[at_z(off) * 2 + c, :, lanes(row)]
+        return rem_copy(
+            ref, ref, sem_as.at[2 + way, i], sem_ar.at[2 + way, i], {"head": lax.rem(y + step + ny, ny)}
+        )
+
+    def take_far(off):
+        z_copy(-off if off != half_z else off, at_z(off) * 2 + c).wait_recv()
+        for way in range(3):
+            start(y_quarter(off, way, y))
+
+    def take_rest(off):
+        if off in far:
+            for way in range(3):
+                y_quarter(off, way, y - (1, -1, 2)[way]).wait_recv()
+        else:
+            z_copy(-off if off != half_z else off, at_z(off) * 2 + c).wait_recv()
+        start(sib_block(off, c))
 
     def pos_copy(d, slot):
         return rem_copy(
             posbuf.at[slot], posbuf.at[slot], sem_ps.at[d], sem_pr.at[d], {"ctx": lax.rem(me + d, nc)}
         )
 
-    start(gather_copy(me, 0, 1))
-    if half_z > 1:
-        start(gather_copy(me, 1, 1))
-    start(gather_copy(me, 2, 0))
     for d in range(1, nc):
         start(pos_copy(d, me))
+    start(sib_block(0, c))
+    for off in reversed(offsets[1:]):
+        start(z_copy(off, me))
 
     fi = lax.broadcasted_iota(jnp.int32, (128, 128), 0)
     fj = lax.broadcasted_iota(jnp.int32, (128, 128), 1)
+    for load in loads[4:]:
+        load.wait()
     for h in range(8):
         part = dot(qn_ref[0, :, 128 * h : 128 * h + 128], ku_ref[h]).astype(BF16)
         qlat[0, 64 * h : 64 * h + 64, :] = part[0:64]
@@ -144,21 +186,13 @@
             for d in range(1, nc):
                 pos_copy(d, lax.rem(me - d + nc, nc)).wait_recv()
         else:
-            block = at_z(-t) * 2 + c
-            gather_copy(block, 0, t).wait_recv()
-            if t < half_z:
-                start(gather_copy(block, 0, t + 1))
-            start(gather_copy(block, 2, t))
-            if t < half_z:
-                block = at_z(t) * 2 + c
-                gather_copy(block, 1, t).wait_recv()
-                if t + 1 < half_z:
-                    start(gather_copy(block, 1, t + 1))
-                start(gather_copy(block, 2, half_z + t))
-        other = 1 - c
-        gather_copy(at_z(-t) * 2 + other, 2, t).wait_recv()
-        if 0 < t < half_z:
-            gather_copy(at_z(t) * 2 + other, 2, half_z + t).wait_recv()
+            if t == 1:
+                for off in far:
+                    take_far(off)
+            for off in g:
+                take_rest(off)
+        for off in g:
+            sib_block(off, 1 - c).wait_recv()
 
         blocks = blocks_of(g)
         n = 64 * len(blocks)
@@ -209,36 +243,36 @@
             psib.at[index], rsib.at[index], sem_ss.at[index], sem_sr.at[index], {"ctx": sib}
         )
 
-    def ring_copy(way, step):
-        src, dst, dev = ((sendp, recvp, up), (sendm, recvm, down))[way]
-        return rem_copy(
-            src.at[step], dst.at[step], sem_zs.at[way, step], sem_zr.at[way, step], {"ctx": dev}
-        )
-
-    index_of = {off: i for i, off in enumerate(off for g in groups for off in g)}
-
-    def summed(off):
-        i = index_of[off]
-        return pown[i].astype(F32) + rsib[i].astype(F32)
+    def z_part(i):
+        return rem_copy(
+            zout.at[i], zin.at[i], sem_zs.at[0, i], sem_zr.at[0, i], {"ctx": at_z(offsets[i]) * 2 + c}
+        )
+
+    cuts = [cut for cut in ([t for t in range(3, half_z + 1)], [2], [0, 1]) if cut and cut[0] <= half_z]
+
+    def y_part(k, d):
+        begin = index_of[groups[cuts[k][0]][0]]
+        size = sum(len(groups[t]) for t in cuts[k])
+        peer = lax.rem(y + d, ny)
+        return rem_copy(
+            yout.at[peer, pl.ds(begin, size)], yin.at[d - 1, pl.ds(begin, size)],
+            sem_ys.at[k, d], sem_yr.at[k, d], {"head": peer},
+        )
 
     def send_on(t):
         for off in groups[t]:
-            sib_copy(index_of[off]).wait_recv()
-        step = half_z - t
-        total = summed(t)
-        if step > 0:
-            ring_copy(0, step - 1).wait_recv()
-            total = total + recvp[step - 1].astype(F32)
-        sendp[step] = total.astype(BF16)
-        start(ring_copy(0, step))
-        if t < half_z:
-            step = half_z - 1 - t
-            total = summed(-t)
-            if step > 0:
-                ring_copy(1, step - 1).wait_recv()
-                total = total + recvm[step - 1].astype(F32)
-            sendm[step] = total.astype(BF16)
-            start(ring_copy(1, step))
+            i = index_of[off]
+            sib_copy(i).wait_recv()
+            total = (pown[i].astype(F32) + rsib[i].astype(F32)).astype(BF16)
+            zout[i] = total[0:160]
+            if off != 0:
+                start(z_part(i))
+            for k in range(ny):
+                yout[k, i] = total[160 + 16 * k : 176 + 16 * k]
+        for k, cut in enumerate(cuts):
+            if cut[0] == t:
+                for d in range(1, ny):
+                    start(y_part(k, d))
 
     gain_acc = jnp.zeros((1, 512), F32)
     for t in reversed(range(len(groups))):
@@ -272,10 +306,14 @@
             index = index_of[g[i // 2]]
 
             def put(buf):
-                buf[index, 0:64, :] = lat_low[64 * i : 64 * i + 64]
-                buf[index, 64:128, :] = lat_high[64 * i : 64 * i + 64]
+                buf[index, 0:64, :] = lat_low[64 * i : 64 * i + 64, 0:256]
+                buf[index, 64:128, :] = lat_high[64 * i : 64 * i + 64, 0:256]
                 for k in range(4):
-                    buf[index, 128:144, 128 * k : 128 * k + 128] = rope[64 * i + 16 * k : 64 * i + 16 * k + 16]
+                    buf[index, 128 + 16 * (k // 2) : 144 + 16 * (k // 2), 128 * (k % 2) : 128 * (k % 2) + 128] = rope[
+                        64 * i + 16 * k : 64 * i + 16 * k + 16
+                    ]
+                buf[index, 160:224, :] = lat_low[64 * i : 64 * i + 64, 256:512]
+                buf[index, 224:288, :] = lat_high[64 * i : 64 * i + 64, 256:512]
 
             @pl.when(c == i % 2)
             def _():
@@ -314,43 +352,60 @@
         return jnp.sum(buf[...], axis=0)
 
     gain_send(0)
+    send_on(0)
     gsend[1] = gain_sum(0)
     gain_send(1)
 
-    sib_copy(0).wait_recv()
-    total = summed(0)
-    ring_copy(0, half_z - 1).wait_recv()
-    total = total + recvp[half_z - 1].astype(F32)
-    if half_z > 1:
-        ring_copy(1, half_z - 2).wait_recv()
-        total = total + recvm[half_z - 2].astype(F32)
+    total = zout[0].astype(F32)
+    for i in range(1, nz):
+        z_part(i).wait_recv()
+        total = total + zin[i].astype(F32)
+    total = total.astype(BF16)
     for k in range(ny):
         q = k % 4
-        ysend[k, :, 0:512] = total[16 * k : 16 * k + 16, :].astype(BF16)
-        ysend[k, :, 512:640] = total[128:144, 128 * q : 128 * q + 128].astype(BF16)
-
-    def y_copy(d, slot):
+        yout2[k, :, 0:256] = total[16 * k : 16 * k + 16]
+        yout2[k, :, 256:384] = total[128 + 16 * (q // 2) : 144 + 16 * (q // 2), 128 * (q % 2) : 128 * (q % 2) + 128]
+
+    def y_last(d):
         peer = lax.rem(y + d, ny)
-        return rem_copy(
-            ysend.at[peer], yrecv.at[slot], sem_ys.at[d - 1], sem_yr.at[d - 1], {"head": peer}
-        )
+        return rem_copy(yout2.at[peer], yin2.at[d], sem_ys.at[3, d], sem_yr.at[3, d], {"head": peer})
 
     for d in range(1, ny):
-        start(y_copy(d, y))
-    yrecv[y] = ysend[y]
+        start(y_last(d))
     gsend[2] = gain_sum(1)
     gain_send(2)
+
+    def z_last(i):
+        return rem_copy(
+            zout2.at[i], zin2.at[i], sem_zs.at[1, i], sem_zr.at[1, i], {"ctx": at_z(offsets[i]) * 2 + c}
+        )
+
+    for k in range(len(cuts)):
+        for d in range(1, ny):
+            y_part(k, d).wait_recv()
+    right = yout[y].astype(F32)
     for d in range(1, ny):
-        y_copy(d, lax.rem(y - d + ny, ny)).wait_recv()
-    mine = jnp.sum(yrecv[...].astype(F32), axis=0)
-
-    cot = mine[:, 0:512]
+        right = right + yin[d - 1].astype(F32)
+    zout2[...] = right.astype(BF16)
+    for i in range(1, nz):
+        start(z_last(i))
+
+    left = yout2[y].astype(F32)
+    for d in range(1, ny):
+        y_last(d).wait_recv()
+        left = left + yin2[d].astype(F32)
+    right = zout2[0].astype(F32)
+    for i in range(1, nz):
+        z_last(i).wait_recv()
+        right = right + zin2[i].astype(F32)
+
+    cot = jnp.concatenate([left[:, 0:256], right], axis=1)
     own = x_ref[0, pl.ds(pl.multiple_of(16 * y, 16), 16), :].astype(F32)
     own_rms = jnp.sqrt(jnp.mean(own * own, axis=-1, keepdims=True) + 1e-06)
     xhat = own / own_rms
     scaled = gain_ref[...] * cot
     raw_ref[0] = (scaled - xhat * jnp.mean(scaled * xhat, axis=-1, keepdims=True)) / own_rms
-    both = mine[:, 512:640]
+    both = left[:, 256:384]
     rope_ref[0] = jnp.where(y >= ny // 2, pltpu.roll(both, 64, 1), both)[:, 0:64]
 
     gout_ref[...] = gain_sum(2) / gain_ref[...] * (1.0 / math.sqrt(total_rows))
@@ -372,47 +427,59 @@
                 jax.ShapeDtypeStruct((1, 16, 64), F32),
                 jax.ShapeDtypeStruct((1, 512), F32),
             ),
-            in_specs=[pl.BlockSpec(memory_space=pltpu.VMEM)] * 9,
+            in_specs=[pl.BlockSpec(memory_space=pl.ANY)] * 9,
             out_specs=[pl.BlockSpec(memory_space=pltpu.VMEM)] * 3,
             scratch_shapes=[
+                pltpu.VMEM((1, 128), jnp.int32),
+                pltpu.VMEM((1, 128, 512), BF16),
+                pltpu.VMEM((1, 512), F32),
+                pltpu.VMEM((1, 64, 128), BF16),
+                pltpu.VMEM((1, 128, 1024), BF16),
+                pltpu.VMEM((1, 128, 512), BF16),
+                pltpu.VMEM((8, 128, 512), BF16),
+                pltpu.VMEM((8, 128, 512), BF16),
+                pltpu.VMEM((1, 128, 1024), BF16),
+                dma((9,)),
                 pltpu.VMEM((nc, 144, 512), BF16),
-                pltpu.VMEM((nc, 8, 128), jnp.int32),
+                pltpu.VMEM((nc, 1, 128), jnp.int32),
                 pltpu.VMEM((2, 512, 512), BF16),
                 pltpu.VMEM((2, 512, 512), BF16),
                 pltpu.VMEM((3, 512, 128), BF16),
                 pltpu.VMEM((3, 64 * nc, 512), F32),
                 pltpu.VMEM((3, 64 * nc, 512), F32),
                 pltpu.VMEM((64, 512), jnp.int32),
-                pltpu.VMEM((nz, 144, 512), BF16),
-                pltpu.VMEM((nz, 144, 512), BF16),
-                pltpu.VMEM((nz, 144, 512), BF16),
-                pltpu.VMEM((half_z, 144, 512), BF16),
-                pltpu.VMEM((half_z, 144, 512), BF16),
-                pltpu.VMEM((max(half_z - 1, 1), 144, 512), BF16),
-                pltpu.VMEM((max(half_z - 1, 1), 144, 512), BF16),
-                pltpu.VMEM((ny, 16, 640), BF16),
-                pltpu.VMEM((ny, 16, 640), BF16),
+                pltpu.VMEM((nz, 288, 256), BF16),
+                pltpu.VMEM((nz, 288, 256), BF16),
+                pltpu.VMEM((nz, 288, 256), BF16),
+                pltpu.VMEM((nz, 160, 256), BF16),
+                pltpu.VMEM((nz, 160, 256), BF16),
+                pltpu.VMEM((ny, nz, 16, 256), BF16),
+                pltpu.VMEM((ny, nz, 16, 256), BF16),
+                pltpu.VMEM((ny, 16, 384), BF16),
+                pltpu.VMEM((ny, 16, 384), BF16),
+                pltpu.VMEM((nz, 16, 256), BF16),
+                pltpu.VMEM((nz, 16, 256), BF16),
                 pltpu.VMEM((3, 1, 512), F32),
                 pltpu.VMEM((nx, 1, 512), F32),
                 pltpu.VMEM((ny, 1, 512), F32),
                 pltpu.VMEM((nc, 1, 512), F32),
-                dma((3, nz + 1)),
-                dma((3, nz + 1)),
+                dma((5, nz)),
+                dma((5, nz)),
                 dma((nc,)),
                 dma((nc,)),
                 dma((nz,)),
                 dma((nz,)),
-                dma((2, half_z)),
-                dma((2, half_z)),
-                dma((ny,)),
-                dma((ny,)),
+                dma((2, nz)),
+                dma((2, nz)),
+                dma((4, ny)),
+                dma((4, ny)),
                 dma((nx + ny + nc,)),
                 dma((nx + ny + nc,)),
             ],
             compiler_params=pltpu.CompilerParams(
-                collective_id=0, has_side_effects=True, vmem_limit_bytes=52 * 1024 * 1024
+                collective_id=0, has_side_effects=True, vmem_limit_bytes=60 * 1024 * 1024
             ),
-        )(pos, unnormed, gain.reshape(1, 512), kr, qn, qr, ku, vu, go)
+        )(pos, unnormed, gain.reshape(1, 512), jnp.swapaxes(kr, 1, 2), qn, qr, ku, vu, go)
         return out[0], out[1], out[2].reshape(512)
 
     in_specs = (

time: 84.3 us -> 67.8 us (0.80)
  Pallas kernels: 75.7 us -> 64.3 us
  local copies, waits for them, and re-layouts: 7.56 us -> 2.65 us
    pallas_call x1, Pallas kernels: 75.7 us -> 64.3 us  [per_device(): pl.pallas_call(functools.partial(kernel, nz, ny, nx, nc * 128 * nx), out_...]
    unnamed x18 -> x7, local copies, waits for them, and re-layouts: 7.56 us -> 2.65 us
where the time goes in v2:
time: 67.8 us; the launch traced here: 67.6 us
  Pallas kernels  64.3 us (95%)
  local copies, waits for them, and re-layouts  2.65 us (4%)
    pallas_call x1, Pallas kernels, per_device(): pl.pallas_call(functools.partial(kernel, nz, ny, nx, nc * 128 * nx), out_...  64.3 us
    unnamed x7, local copies, waits for them, and re-layouts  2.65 us

profile of v2, /device:TPU:1, one launch (start us, length us, event | category | flops | bytes accessed | tf_op | source)
XLA Modules:
  0.0 67.6 jit_solution(15464531477306526489)
XLA Ops:
  0.6 64.3 %shard_map.112 = (f32[1,16,512]{2,1,0:T(8,128)}, f32[1,16,64]{2,1,0:T(8,128)}, f32[1,512]{1,0:T(1,128)}) custom-call(s32[1,128]{1,0:T(1,128)} %pos_in.1, bf16[1,128,512]{2,1,0:T(8,128)(2,1)} %x_in.1, f32[1,512]{1,0:T(1,128)} %bitcast.5, bf16[1,64,128]{2,1,0:T(8,128)(2,1)} %bitcast.3, bf16[1,128,1024]{2,1,0:T(8,128)(2,1)} %qn_in.1, ...), custom_call_target="tpu_custom_call" | custom-call | tf_op jit(solution)/shard_map/pallas_call | solution.py:423
  64.9 0.0 copy-start
  64.9 1.4 %copy.15 = f32[1,16,512]{2,1,0:T(8,128)} copy(f32[1,16,512]{2,1,0:T(8,128)} %get-tuple-element.12) | data formatting | bytes 65536
  66.3 0.0 copy-done
  66.3 0.0 copy-start.1
  66.3 0.6 copy.16
  66.9 0.1 copy-done.1
  67.0 0.6 copy.17
Async XLA Ops:
  64.9 1.4 %copy-start = (f32[1,16,64]{2,1,0:T(8,128)S(1)}, f32[1,16,64]{2,1,0:T(8,128)}, u32[]{:S(2)}) copy-start(f32[1,16,64]{2,1,0:T(8,128)} %get-tuple-element.13) | copy-start | bytes 12292
  66.3 0.7 %copy-start.1 = (f32[1,512]{1,0:T(1,128)S(1)}, f32[1,512]{1,0:T(1,128)}, u32[]{:S(2)}) copy-start(f32[1,512]{1,0:T(1,128)} %get-tuple-element.8) | copy-start | bytes 6148

commit v3 on v2

--- a/solution.py
+++ b/solution.py
@@ -50,7 +50,7 @@
     ins = (x_in, kr_in, gain_in, pos_in, qn_in, ku_in, go_in, vu_in, qr_in)
     here = (x_ref, kr_ref, gain_ref, pos_ref, qn_ref, ku_ref, go_ref, vu_ref, qr_ref)
     loads = [pltpu.make_async_copy(a, b, sem_in.at[i]) for i, (a, b) in enumerate(zip(ins, here))]
-    for load in loads:
+    for load in loads[0:4]:
         load.start()
 
     barrier = pltpu.get_barrier_semaphore()
@@ -60,6 +60,9 @@
         pl.semaphore_signal(barrier, inc=1, device_id={"head": lax.rem(y + d, ny)}, device_id_type=MESH)
     for d in range(1, nx):
         pl.semaphore_signal(barrier, inc=1, device_id={"dp": lax.rem(x + d, nx)}, device_id_type=MESH)
+
+    for load in loads[4:]:
+        load.start()
 
     for load in loads[0:4]:
         load.wait()
@@ -129,10 +132,12 @@
             posbuf.at[slot], posbuf.at[slot], sem_ps.at[d], sem_pr.at[d], {"ctx": lax.rem(me + d, nc)}
         )
 
+    for off in far:
+        start(z_copy(off, me))
+    start(sib_block(0, c))
     for d in range(1, nc):
         start(pos_copy(d, me))
-    start(sib_block(0, c))
-    for off in reversed(offsets[1:]):
+    for off in offsets[1:3]:
         start(z_copy(off, me))
 
     fi = lax.broadcasted_iota(jnp.int32, (128, 128), 0)
@@ -183,14 +188,14 @@
     tops = []
     for t, g in enumerate(groups):
         if t == 0:
+            for off in far:
+                take_far(off)
             for d in range(1, nc):
                 pos_copy(d, lax.rem(me - d + nc, nc)).wait_recv()
         else:
-            if t == 1:
-                for off in far:
-                    take_far(off)
-            for off in g:
-                take_rest(off)
+            if t < half_z:
+                for off in g + (groups[t + 1] if t + 1 == half_z else []):
+                    take_rest(off)
         for off in g:
             sib_block(off, 1 - c).wait_recv()
 
@@ -243,36 +248,66 @@
             psib.at[index], rsib.at[index], sem_ss.at[index], sem_sr.at[index], {"ctx": sib}
         )
 
+    relayed = half_z == 4
+    stops = {3: 1, -3: -1, 4: 2 - 4 * c} if relayed else {}
+
     def z_part(i):
-        return rem_copy(
-            zout.at[i], zin.at[i], sem_zs.at[0, i], sem_zr.at[0, i], {"ctx": at_z(offsets[i]) * 2 + c}
-        )
-
-    cuts = [cut for cut in ([t for t in range(3, half_z + 1)], [2], [0, 1]) if cut and cut[0] <= half_z]
+        off = offsets[i]
+        return rem_copy(
+            zout.at[i], zin.at[i], sem_zs.at[0, i], sem_zr.at[0, i], {"ctx": at_z(stops.get(off, off)) * 2 + c}
+        )
+
+    def relay():
+        for off in (3, -3, 4):
+            z_part(index_of[off]).wait_recv()
+        for off, source, core in ((2, 3, 0), (-2, -3, 1)):
+            i = index_of[off]
+            total = pown[i, 0:160].astype(F32) + rsib[i, 0:160].astype(F32) + zin[index_of[source]].astype(F32)
+            zout[i] = (total + jnp.where(c == core, zin[index_of[4]].astype(F32), 0.0)).astype(BF16)
+            start(z_part(i))
+
+    cuts = [[t] for t in range(half_z, -1, -1)]
 
     def y_part(k, d):
         begin = index_of[groups[cuts[k][0]][0]]
         size = sum(len(groups[t]) for t in cuts[k])
         peer = lax.rem(y + d, ny)
+        stop = lax.rem(y + {3: 1, 5: 7, 4: 2 + 4 * c}.get(d, d), ny) if y_relayed(k) else peer
         return rem_copy(
             yout.at[peer, pl.ds(begin, size)], yin.at[d - 1, pl.ds(begin, size)],
-            sem_ys.at[k, d], sem_yr.at[k, d], {"head": peer},
-        )
+            sem_ys.at[k, d], sem_yr.at[k, d], {"head": stop},
+        )
+
+    def y_relayed(k):
+        return ny == 8 and cuts[k][0] > 1
+
+    def y_relay(k):
+        begin = index_of[groups[cuts[k][0]][0]]
+        span = pl.ds(begin, sum(len(groups[t]) for t in cuts[k]))
+        for d in (3, 5, 4):
+            y_part(k, d).wait_recv()
+        for d, source, core in ((2, 3, 0), (6, 5, 1)):
+            peer = lax.rem(y + d, ny)
+            total = yout[peer, span].astype(F32) + yin[source - 1, span].astype(F32)
+            yout[peer, span] = (total + jnp.where(c == core, yin[3, span].astype(F32), 0.0)).astype(BF16)
+            start(y_part(k, d))
 
     def send_on(t):
         for off in groups[t]:
             i = index_of[off]
             sib_copy(i).wait_recv()
             total = (pown[i].astype(F32) + rsib[i].astype(F32)).astype(BF16)
-            zout[i] = total[0:160]
-            if off != 0:
-                start(z_part(i))
+            if not relayed or abs(off) != 2:
+                zout[i] = total[0:160]
+                if off != 0:
+                    start(z_part(i))
             for k in range(ny):
                 yout[k, i] = total[160 + 16 * k : 176 + 16 * k]
         for k, cut in enumerate(cuts):
             if cut[0] == t:
                 for d in range(1, ny):
-                    start(y_part(k, d))
+                    if not (y_relayed(k) and d in (2, 6)):
+                        start(y_part(k, d))
 
     gain_acc = jnp.zeros((1, 512), F32)
     for t in reversed(range(len(groups))):
@@ -353,13 +388,21 @@
 
     gain_send(0)
     send_on(0)
+    if y_relayed(0):
+        y_relay(0)
+    if relayed:
+        relay()
+    for k in range(1, len(cuts)):
+        if y_relayed(k):
+            y_relay(k)
     gsend[1] = gain_sum(0)
     gain_send(1)
 
     total = zout[0].astype(F32)
     for i in range(1, nz):
-        z_part(i).wait_recv()
-        total = total + zin[i].astype(F32)
+        if offsets[i] not in stops:
+            z_part(i).wait_recv()
+            total = total + zin[i].astype(F32)
     total = total.astype(BF16)
     for k in range(ny):
         q = k % 4
@@ -368,7 +411,7 @@
 
     def y_last(d):
         peer = lax.rem(y + d, ny)
-        return rem_copy(yout2.at[peer], yin2.at[d], sem_ys.at[3, d], sem_yr.at[3, d], {"head": peer})
+        return rem_copy(yout2.at[peer], yin2.at[d], sem_ys.at[half_z + 1, d], sem_yr.at[half_z + 1, d], {"head": peer})
 
     for d in range(1, ny):
         start(y_last(d))
@@ -380,13 +423,15 @@
             zout2.at[i], zin2.at[i], sem_zs.at[1, i], sem_zr.at[1, i], {"ctx": at_z(offsets[i]) * 2 + c}
         )
 
-    for k in range(len(cuts)):
+    for k, cut in enumerate(cuts):
+        begin = index_of[groups[cut[0]][0]]
+        span = pl.ds(begin, sum(len(groups[t]) for t in cut))
+        right = yout[y, span].astype(F32)
         for d in range(1, ny):
-            y_part(k, d).wait_recv()
-    right = yout[y].astype(F32)
-    for d in range(1, ny):
-        right = right + yin[d - 1].astype(F32)
-    zout2[...] = right.astype(BF16)
+            if not (y_relayed(k) and d in (3, 4, 5)):
+                y_part(k, d).wait_recv()
+                right = right + yin[d - 1, span].astype(F32)
+        zout2[span] = right.astype(BF16)
     for i in range(1, nz):
         start(z_last(i))
 
@@ -411,6 +456,12 @@
     gout_ref[...] = gain_sum(2) / gain_ref[...] * (1.0 / math.sqrt(total_rows))
     for copy in started:
         copy.wait_send()
+
+
+def hand_over(raw_in, rope_in, gain_in, raw_out, rope_out, gain_out):
+    raw_out[...] = raw_in[...]
+    rope_out[...] = rope_in[...]
+    gain_out[...] = gain_in[...]
 
 
 def solution(mesh):
@@ -427,7 +478,7 @@
                 jax.ShapeDtypeStruct((1, 16, 64), F32),
                 jax.ShapeDtypeStruct((1, 512), F32),
             ),
-            in_specs=[pl.BlockSpec(memory_space=pl.ANY)] * 9,
+            in_specs=[pl.BlockSpec(memory_space=pltpu.HBM)] * 9,
             out_specs=[pl.BlockSpec(memory_space=pltpu.VMEM)] * 3,
             scratch_shapes=[
                 pltpu.VMEM((1, 128), jnp.int32),
@@ -471,8 +522,8 @@
                 dma((nz,)),
                 dma((2, nz)),
                 dma((2, nz)),
-                dma((4, ny)),
-                dma((4, ny)),
+                dma((half_z + 2, ny)),
+                dma((half_z + 2, ny)),
                 dma((nx + ny + nc,)),
                 dma((nx + ny + nc,)),
             ],
@@ -480,6 +531,12 @@
                 collective_id=0, has_side_effects=True, vmem_limit_bytes=60 * 1024 * 1024
             ),
         )(pos, unnormed, gain.reshape(1, 512), jnp.swapaxes(kr, 1, 2), qn, qr, ku, vu, go)
+        out = pl.pallas_call(
+            hand_over,
+            out_shape=tuple(jax.ShapeDtypeStruct(o.shape, F32) for o in out),
+            in_specs=[pl.BlockSpec(memory_space=pltpu.VMEM)] * 3,
+            out_specs=[pl.BlockSpec(memory_space=pltpu.VMEM)] * 3,
+        )(*out)
         return out[0], out[1], out[2].reshape(512)
 
     in_specs = (

time: 67.8 us -> 63.1 us (0.931)
  local copies, waits for them, and re-layouts: 2.65 us -> 0 us
  Pallas kernels: 64.3 us -> 62.3 us
    pallas_call x1, Pallas kernels: 64.3 us -> 60.9 us  [per_device(): pl.pallas_call(functools.partial(kernel, nz, ny, nx, nc * 128 * nx), out_...]
    unnamed x7 -> x0, local copies, waits for them, and re-layouts: 2.65 us -> none
    pallas_call x0 -> x1, Pallas kernels: none -> 1.4 us  [per_device(): pl.pallas_call(hand_over, out_shape=tuple((jax.ShapeDtypeStruct(o.shape,...]
where the time goes in v3:
time: 63.1 us; the launch traced here: 62.9 us
  Pallas kernels  62.3 us (99%)
  between operations  0.64 us (1%)
    pallas_call x1, Pallas kernels, per_device(): pl.pallas_call(functools.partial(kernel, nz, ny, nx, nc * 128 * nx), out_...  60.9 us
    pallas_call x1, Pallas kernels, per_device(): pl.pallas_call(hand_over, out_shape=tuple((jax.ShapeDtypeStruct(o.shape,...  1.4 us

profile of v3, /device:TPU:1, one launch (start us, length us, event | category | flops | bytes accessed | tf_op | source)
XLA Modules:
  0.0 62.9 jit_solution(17921503244600372744)
XLA Ops:
  0.6 60.9 %shard_map.112 = (f32[1,16,512]{2,1,0:T(8,128)}, f32[1,16,64]{2,1,0:T(8,128)}, f32[1,512]{1,0:T(1,128)}) custom-call(s32[1,128]{1,0:T(1,128)} %pos_in.1, bf16[1,128,512]{2,1,0:T(8,128)(2,1)} %x_in.1, f32[1,512]{1,0:T(1,128)} %bitcast.4, bf16[1,64,128]{2,1,0:T(8,128)(2,1)} %bitcast.3, bf16[1,128,1024]{2,1,0:T(8,128)(2,1)} %qn_in.1, ...), custom_call_target="tpu_custom_call" | custom-call | tf_op jit(solution)/shard_map/pallas_call | solution.py:474
  61.5 1.4 %shard_map.113 = (f32[1,16,512]{2,1,0:T(8,128)}, f32[1,16,64]{2,1,0:T(8,128)}, f32[1,512]{1,0:T(1,128)}) custom-call(f32[1,16,512]{2,1,0:T(8,128)} %get-tuple-element.9.raw_in, f32[1,16,64]{2,1,0:T(8,128)} %get-tuple-element.10.rope_in, f32[1,512]{1,0:T(1,128)} %get-tuple-element.11.gain_in), custom_call_target="tpu_custom_call" | custom-call | tf_op jit(solution)/shard_map/pallas_call | solution.py:534

commit v4 on v3

--- a/solution.py
+++ b/solution.py
@@ -185,16 +185,25 @@
     m_lo = m_up
     l_up = jnp.zeros((1, 512), F32)
     l_lo, d_up, d_lo = l_up, l_up, l_up
-    tops = []
-    for t, g in enumerate(groups):
+    tops = {}
+    order = [0, 2, 1, 3, 4] if half_z == 4 else list(range(half_z + 1))
+    for t in order:
+        g = groups[t]
         if t == 0:
-            for off in far:
+            for off in far[0:2]:
                 take_far(off)
-            for d in range(1, nc):
+            pos_copy(jnp.where(c == 1, 1, nc - 1), sib).wait_recv()
+        else:
+            if t == order[1]:
+                for off in far[2:]:
+                    take_far(off)
+                for d in range(2, nc - 1):
+                    pos_copy(d, lax.rem(me - d + nc, nc)).wait_recv()
+                d = jnp.where(c == 1, nc - 1, 1)
                 pos_copy(d, lax.rem(me - d + nc, nc)).wait_recv()
-        else:
-            if t < half_z:
-                for off in g + (groups[t + 1] if t + 1 == half_z else []):
+            ahead = {1: [1, 3], 3: [4], 4: []} if half_z == 4 else {}
+            for other in ahead.get(t, [t]):
+                for off in groups[other]:
                     take_rest(off)
         for off in g:
             sib_block(off, 1 - c).wait_recv()
@@ -228,7 +237,7 @@
         a_lo = jnp.exp2(m_lo - new_lo)
         m_up, m_lo = new_up, new_lo
         l_up, d_up, l_lo, d_lo = l_up * a_up, d_up * a_up, l_lo * a_lo, d_lo * a_lo
-        tops.append((m_up, m_lo))
+        tops[t] = (m_up, m_lo)
         for kind in range(3):
             top = m_lo if kind == 2 else m_up
             w = jnp.exp2(wbuf[kind, span, :] - top)
@@ -390,13 +399,15 @@
     send_on(0)
     if y_relayed(0):
         y_relay(0)
+    gsend[1] = gain_sum(0)
+    gain_send(1)
     if relayed:
         relay()
     for k in range(1, len(cuts)):
         if y_relayed(k):
             y_relay(k)
-    gsend[1] = gain_sum(0)
-    gain_send(1)
+    gsend[2] = gain_sum(1)
+    gain_send(2)
 
     total = zout[0].astype(F32)
     for i in range(1, nz):
@@ -415,8 +426,6 @@
 
     for d in range(1, ny):
         start(y_last(d))
-    gsend[2] = gain_sum(1)
-    gain_send(2)
 
     def z_last(i):
         return rem_copy(

time: 63.1 us -> 60.5 us (0.959)
  Pallas kernels: 62.3 us -> 59.4 us
    pallas_call x1, Pallas kernels: 60.9 us -> 58 us  [per_device(): pl.pallas_call(functools.partial(kernel, nz, ny, nx, nc * 128 * nx), out_...]
where the time goes in v4:
time: 60.5 us; the launch traced here: 60 us
  Pallas kernels  59.4 us (98%)
  between operations  0.64 us (1%)
    pallas_call x1, Pallas kernels, per_device(): pl.pallas_call(functools.partial(kernel, nz, ny, nx, nc * 128 * nx), out_...  58 us
    pallas_call x1, Pallas kernels, per_device(): pl.pallas_call(hand_over, out_shape=tuple((jax.ShapeDtypeStruct(o.shape,...  1.4 us

profile of v4, /device:TPU:1, one launch (start us, length us, event | category | flops | bytes accessed | tf_op | source)
XLA Modules:
  0.0 60.0 jit_solution(2938859780488032293)
XLA Ops:
  0.6 58.0 %shard_map.112 = (f32[1,16,512]{2,1,0:T(8,128)}, f32[1,16,64]{2,1,0:T(8,128)}, f32[1,512]{1,0:T(1,128)}) custom-call(s32[1,128]{1,0:T(1,128)} %pos_in.1, bf16[1,128,512]{2,1,0:T(8,128)(2,1)} %x_in.1, f32[1,512]{1,0:T(1,128)} %bitcast.4, bf16[1,64,128]{2,1,0:T(8,128)(2,1)} %bitcast.3, bf16[1,128,1024]{2,1,0:T(8,128)(2,1)} %qn_in.1, ...), custom_call_target="tpu_custom_call" | custom-call | tf_op jit(solution)/shard_map/pallas_call | solution.py:483
  58.6 1.4 %shard_map.113 = (f32[1,16,512]{2,1,0:T(8,128)}, f32[1,16,64]{2,1,0:T(8,128)}, f32[1,512]{1,0:T(1,128)}) custom-call(f32[1,16,512]{2,1,0:T(8,128)} %get-tuple-element.9.raw_in, f32[1,16,64]{2,1,0:T(8,128)} %get-tuple-element.10.rope_in, f32[1,512]{1,0:T(1,128)} %get-tuple-element.11.gain_in), custom_call_target="tpu_custom_call" | custom-call | tf_op jit(solution)/shard_map/pallas_call | solution.py:543

commit v5 on v4

--- a/solution.py
+++ b/solution.py
@@ -399,13 +399,14 @@
     send_on(0)
     if y_relayed(0):
         y_relay(0)
-    gsend[1] = gain_sum(0)
-    gain_send(1)
     if relayed:
         relay()
     for k in range(1, len(cuts)):
         if y_relayed(k):
             y_relay(k)
+        if k == 1:
+            gsend[1] = gain_sum(0)
+            gain_send(1)
     gsend[2] = gain_sum(1)
     gain_send(2)
 

time: 60.5 us -> 60.7 us (level)
  no operation moved by 1% of the time
where the time goes in v5:
time: 60.7 us; the launch traced here: 60.4 us
  Pallas kernels  59.8 us (99%)
  between operations  0.64 us (1%)
    pallas_call x1, Pallas kernels, per_device(): pl.pallas_call(functools.partial(kernel, nz, ny, nx, nc * 128 * nx), out_...  58.4 us
    pallas_call x1, Pallas kernels, per_device(): pl.pallas_call(hand_over, out_shape=tuple((jax.ShapeDtypeStruct(o.shape,...  1.4 us

profile of v5, /device:TPU:1, one launch (start us, length us, event | category | flops | bytes accessed | tf_op | source)
XLA Modules:
  0.0 60.4 jit_solution(5439557828280801409)
XLA Ops:
  0.6 58.4 %shard_map.112 = (f32[1,16,512]{2,1,0:T(8,128)}, f32[1,16,64]{2,1,0:T(8,128)}, f32[1,512]{1,0:T(1,128)}) custom-call(s32[1,128]{1,0:T(1,128)} %pos_in.1, bf16[1,128,512]{2,1,0:T(8,128)(2,1)} %x_in.1, f32[1,512]{1,0:T(1,128)} %bitcast.4, bf16[1,64,128]{2,1,0:T(8,128)(2,1)} %bitcast.3, bf16[1,128,1024]{2,1,0:T(8,128)(2,1)} %qn_in.1, ...), custom_call_target="tpu_custom_call" | custom-call | tf_op jit(solution)/shard_map/pallas_call | solution.py:484
  59.0 1.4 %shard_map.113 = (f32[1,16,512]{2,1,0:T(8,128)}, f32[1,16,64]{2,1,0:T(8,128)}, f32[1,512]{1,0:T(1,128)}) custom-call(f32[1,16,512]{2,1,0:T(8,128)} %get-tuple-element.9.raw_in, f32[1,16,64]{2,1,0:T(8,128)} %get-tuple-element.10.rope_in, f32[1,512]{1,0:T(1,128)} %get-tuple-element.11.gain_in), custom_call_target="tpu_custom_call" | custom-call | tf_op jit(solution)/shard_map/pallas_call | solution.py:544
